TPU v7x, 32 devices: a whole 2x2x4 slice. The times are simulated.
32 devices in a mesh: groups: 1, seq: 32 (over z, y, x, core).
Axes of the slice: x: 2, y: 2, z: 4, core: 2. Of those that a mesh axis runs over, the one named last changes fastest.
Arguments:
- token_ids: int32 [65536], P(('groups', 'seq')), may hold values from 0 to 30521
- embed_table: bfloat16 [1024, 30522], P('seq'), may hold values from -6 to 6
- right_blocks: bfloat16 [256, 256, 256], P('seq'), may hold values from -0.5 to 0.5
- right_pattern: int32 [256, 2, 2], P('seq'), may hold values 0 or 1
- left_blocks: bfloat16 [256, 256, 256], P('seq'), may hold values from -0.5 to 0.5
- left_pattern: int32 [256, 2, 2], P('seq'), may hold values 0 or 1
- value_gain: float32 [1024], replicated, may hold values from 0.1 to 1.9
- gate_gain: float32 [1024], replicated, may hold values from 0.1 to 1.9
- cotangent: bfloat16 [65536, 1024], P(('groups', 'seq')), may hold values from -0.375 to 0.375
Outputs:
- grad_right: bfloat16 [256, 256, 256], P(('groups', 'seq'))
- grad_left: bfloat16 [256, 256, 256], P(('groups', 'seq'))
- grad_value_gain: float32 [1024], P('groups')
- grad_gate_gain: float32 [1024], P('groups')
Inputs may be any that keep to these rules, and one draw needn't show every extreme that they name: `right_pattern`: entry (b, r, s) is 1 where tile (r, s) of block b may be nonzero. `left_pattern`: entry (b, r, s) is 1 where tile (r, s) of block b may be nonzero.
All inputs are finite; a program needn't handle non-finite values.
Results may differ from a plain program's by a relative error of at most 0.0065.
Values may be sent and summed in bfloat16 or wider, within the bound.
A program may use at most 128 MiB of HBM per device.

v0:
```python
import jax
import jax.numpy as jnp
from jax import lax
from jax.sharding import PartitionSpec as P


def expand_pattern(pattern, tile_size):
    return jnp.repeat(jnp.repeat(pattern, tile_size, axis=1), tile_size, axis=2).astype(
        jnp.bfloat16
    )


def local(
    token_ids,
    embed_table,
    right_blocks,
    right_pattern,
    left_blocks,
    left_pattern,
    value_gain,
    gate_gain,
    cotangent,
):
    local_rows = right_blocks.shape[0]
    grid_side = right_blocks.shape[1]
    channels = value_gain.shape[0]
    tile_size = grid_side // right_pattern.shape[1]
    every_id = lax.all_gather(token_ids, "seq", axis=0, tiled=True)
    looked_up = jnp.take(embed_table, every_id, axis=1)
    features = lax.all_to_all(looked_up, "seq", split_axis=1, concat_axis=0, tiled=True)
    x_grid = features.T.reshape(local_rows, grid_side, channels)
    values = (x_grid.astype(jnp.float32) * value_gain).astype(jnp.bfloat16)
    right_mask = expand_pattern(right_pattern, tile_size)
    right_eff = right_blocks * right_mask
    row_mixed = jnp.einsum(
        "ikj,ijc->ikc", right_eff, values, preferred_element_type=jnp.float32
    ).astype(jnp.bfloat16)
    column_view = lax.all_to_all(row_mixed, "seq", split_axis=1, concat_axis=0, tiled=True)
    left_mask = expand_pattern(left_pattern, tile_size)
    left_eff = left_blocks * left_mask
    mixed = jnp.einsum(
        "kai,ikc->akc", left_eff, column_view, preferred_element_type=jnp.float32
    ).astype(jnp.bfloat16)
    grad_grid = cotangent.reshape(local_rows, grid_side, channels)
    mixed_rows = lax.all_to_all(mixed, "seq", split_axis=0, concat_axis=1, tiled=True)
    inputs_f32 = x_grid.astype(jnp.float32)
    gate_value = jax.nn.sigmoid(inputs_f32 * gate_gain)
    grad_f32 = grad_grid.astype(jnp.float32)
    gate_term = jnp.sum(
        grad_f32 * mixed_rows.astype(jnp.float32) * gate_value * (1.0 - gate_value) * inputs_f32,
        axis=(0, 1),
    )
    grad_mixed_rows = (grad_f32 * gate_value).astype(jnp.bfloat16)
    grad_mixed = lax.all_to_all(grad_mixed_rows, "seq", split_axis=1, concat_axis=0, tiled=True)
    grad_left = (
        jnp.einsum("akc,ikc->kai", grad_mixed, column_view, preferred_element_type=jnp.float32)
        * left_mask.astype(jnp.float32)
    ).astype(jnp.bfloat16)
    grad_row_cols = jnp.einsum(
        "kai,akc->ikc", left_eff, grad_mixed, preferred_element_type=jnp.float32
    ).astype(jnp.bfloat16)
    grad_row_mixed = lax.all_to_all(grad_row_cols, "seq", split_axis=0, concat_axis=1, tiled=True)
    grad_values = jnp.einsum(
        "ikj,ikc->ijc", right_eff, grad_row_mixed, preferred_element_type=jnp.float32
    )
    grad_right = (
        jnp.einsum("ikc,ijc->ikj", grad_row_mixed, values, preferred_element_type=jnp.float32)
        * right_mask.astype(jnp.float32)
    ).astype(jnp.bfloat16)
    value_term = jnp.sum(grad_values * x_grid.astype(jnp.float32), axis=(0, 1))
    grad_value_gain, grad_gate_gain = lax.psum((value_term, gate_term), "seq")
    return (grad_right, grad_left, grad_value_gain, grad_gate_gain)


def solution(mesh):
    return jax.shard_map(
        local,
        mesh=mesh,
        in_specs=(
            P(("groups", "seq")),
            P("seq", None),
            P("seq", None, None),
            P("seq", None, None),
            P("seq", None, None),
            P("seq", None, None),
            P(),
            P(),
            P(("groups", "seq"), None),
        ),
        out_specs=(
            P(("groups", "seq"), None, None),
            P(("groups", "seq"), None, None),
            P("groups"),
            P("groups"),
        ),
        check_vma=False,
    )
```

profile of v0, /device:TPU:12, one launch (start us, length us, event | category | flops | bytes accessed | tf_op | source)
XLA Modules:
  0.0 884.6 jit_solution(12722908701160563943)
XLA Ops:
  0.6 32.7 %all_gather.3 = s32[65536]{0:T(1024)S(1)} all-gather(s32[2048]{0:T(1024)} %param.9), channel_id=1, replica_groups=mesh['groups'=1,'seq'=32] {'seq'}, dimensions={0}, use_global_device_ids=true | all-gather | bytes 270336 | tf_op jit(solution)/shard_map/all_gather | solution.py:28
  33.3 0.1 fusion.31
  33.4 0.1 compare_and_fusion
  33.5 7.1 copy.80
  40.6 223.6 %gather_fusion = bf16[65536,32]{1,0:T(8,128)(2,1)} fusion(bf16[32,30522]{0,1:T(8,128)(2,1)} %copy.80, s32[65536]{0:T(1024)S(1)} %fusion.31), kind=kCustom, calls=%fused_computation | custom fusion | bytes 8650752 | tf_op jit(solution)/shard_map/jit(_take)/gather | solution.py:29
  264.2 14.9 %copy.81 = bf16[32,32,2048]{2,0,1:T(8,128)(2,1)} copy(bf16[32,32,2048]{0,2,1:T(8,128)(2,1)} %bitcast.57) | data formatting | bytes 8388608 | tf_op jit(solution)/shard_map/jit(_take)/gather | solution.py:29
  279.2 0.1 broadcast_in_dim.28
  279.2 4.6 broadcast_select_fusion
  283.9 13.6 %all-to-all-start = ((bf16[32,32,2048]{2,0,1:T(8,128)(2,1)}), bf16[32,32,2048]{2,0,1:T(8,128)(2,1)}, u32[]{:S(2)}, u32[]{:S(2)}) async-start(bf16[32,32,2048]{2,0,1:T(8,128)(2,1)} %broadcast_select_fusion), calls=%async_computation | async-start | bytes 8388608 | tf_op jit(solution)/shard_map/all_to_all | solution.py:30
  297.5 6.5 copy.78
  304.1 6.9 copy.79
  310.9 77.2 %all-to-all-done = bf16[32,32,2048]{2,0,1:T(8,128)(2,1)} async-done(((bf16[32,32,2048]{2,0,1:T(8,128)(2,1)}), bf16[32,32,2048]{2,0,1:T(8,128)(2,1)}, u32[]{:S(2)}, u32[]{:S(2)}) %all-to-all-start) | async-done | bytes 4194336 | tf_op jit(solution)/shard_map/all_to_all | solution.py:30
  388.1 6.5 convert_element_type.140
  394.6 9.3 %copy.82 = f32[2048,1024]{1,0:T(8,128)} copy(f32[2048,1024]{0,1:T(8,128)} %bitcast.56) | data formatting | bytes 16777216 | tf_op jit(solution)/shard_map/convert_element_type | solution.py:46
  403.9 7.0 multiply_convert_fusion.1
  410.9 4.3 copy.83
  415.2 7.9 all-to-all-start.1
  423.1 0.1 copy.90
  423.2 0.1 broadcast_in_dim.34
  423.3 2.5 broadcast_in_dim.35
  425.8 0.7 convert_element_type.116
  426.5 4.7 convolution_convert_fusion
  431.2 4.3 copy.91
  435.4 78.0 %all-to-all-done.1 = bf16[8,256,1024]{2,0,1:T(8,128)(2,1)} async-done(((bf16[8,256,1024]{2,0,1:T(8,128)(2,1)}), bf16[8,256,1024]{2,0,1:T(8,128)(2,1)}, u32[]{:S(2)}, u32[]{:S(2)}) %all-to-all-start.1) | async-done | bytes 4194336 | tf_op jit(solution)/shard_map/all_to_all | solution.py:54
  513.5 7.4 all-to-all-start.3
  520.9 0.1 copy.86
  521.0 0.1 broadcast_in_dim.32
  521.0 2.5 broadcast_in_dim.33
  523.5 0.7 convert_element_type.110
  524.2 6.6 copy.85
  530.9 1.9 copy-done
  532.8 7.2 convert_bitcast_fusion.2
  540.0 6.8 copy.88
  546.8 64.7 %all-to-all-done.3 = bf16[8,256,1024]{2,0,1:T(8,128)(2,1)} async-done(((bf16[8,256,1024]{2,0,1:T(8,128)(2,1)}), bf16[8,256,1024]{2,0,1:T(8,128)(2,1)}, u32[]{:S(2)}, u32[]{:S(2)}) %all-to-all-start.3) | async-done | bytes 4194336 | tf_op jit(solution)/shard_map/all_to_all | solution.py:38
  611.5 16.6 %all-to-all-start.2 = ((bf16[256,8,1024]{2,1,0:T(8,128)(2,1)}), bf16[256,8,1024]{2,1,0:T(8,128)(2,1)}, u32[]{:S(2)}, u32[]{:S(2)}) async-start(bf16[256,8,1024]{2,1,0:T(8,128)(2,1)} %copy.88), calls=%async_computation.2 | async-start | bytes 8388608 | tf_op jit(solution)/shard_map/all_to_all | solution.py:62
  628.1 5.6 convert_bitcast_fusion.1
  633.7 6.8 copy.96
  640.5 78.0 %all-to-all-done.2 = bf16[256,8,1024]{2,1,0:T(8,128)(2,1)} async-done(((bf16[256,8,1024]{2,1,0:T(8,128)(2,1)}), bf16[256,8,1024]{2,1,0:T(8,128)(2,1)}, u32[]{:S(2)}, u32[]{:S(2)}) %all-to-all-start.2) | async-done | bytes 4194336 | tf_op jit(solution)/shard_map/all_to_all | solution.py:62
  718.5 7.4 all-to-all-start.4
  725.9 7.4 multiply_convert_fusion.2
  733.2 6.1 multiply_reduce_fusion.1
  739.3 7.0 multiply_convert_fusion.3
  746.3 70.1 %all-to-all-done.4 = bf16[256,8,1024]{2,1,0:T(8,128)(2,1)} async-done(((bf16[256,8,1024]{2,1,0:T(8,128)(2,1)}), bf16[256,8,1024]{2,1,0:T(8,128)(2,1)}, u32[]{:S(2)}, u32[]{:S(2)}) %all-to-all-start.4) | async-done | bytes 4194336 | tf_op jit(solution)/shard_map/all_to_all | solution.py:45
  816.5 3.2 convert_bitcast_fusion
  819.7 4.1 copy.97
  823.8 9.3 %copy.98 = f32[2048,1024]{0,1:T(8,128)} copy(f32[2048,1024]{1,0:T(8,128)} %bitcast.55) | data formatting | bytes 16777216 | tf_op jit(solution)/shard_map/convert_element_type | solution.py:50
  833.1 7.8 multiply_reduce_fusion
  840.9 43.5 %all-reduce = (f32[1024]{0:T(1024)}, f32[1024]{0:T(1024)}) all-reduce(f32[1024]{0:T(1024)S(1)} %multiply_reduce_fusion.1, f32[1024]{0:T(1024)S(1)} %multiply_reduce_fusion), channel_id=1, replica_groups=mesh['groups'=1,'seq'=32] {'seq'}, use_global_device_ids=true, to_apply=%region_1.2 | all-reduce | flops 2048 | bytes 16384 | tf_op jit(solution)/shard_map/psum | solution.py:71
  (17 shorter events, 0.0 us)
Async XLA Ops:
  283.9 104.2 %all-to-all-start = ((bf16[32,32,2048]{2,0,1:T(8,128)(2,1)}), bf16[32,32,2048]{2,0,1:T(8,128)(2,1)}, u32[]{:S(2)}, u32[]{:S(2)}) async-start(bf16[32,32,2048]{2,0,1:T(8,128)(2,1)} %broadcast_select_fusion), calls=%async_computation | async-start | bytes 8388608 | tf_op jit(solution)/shard_map/all_to_all | solution.py:30
  394.6 9.3 %copy-start.5 = (f32[1024]{0:T(1024)S(1)}, f32[1024]{0:T(1024)}, u32[]{:S(2)}) copy-start(f32[1024]{0:T(1024)} %param.16) | copy-start | bytes 12292
  415.2 7.9 copy-start.6
  415.2 98.3 %all-to-all-start.1 = ((bf16[8,256,1024]{2,0,1:T(8,128)(2,1)}), bf16[8,256,1024]{2,0,1:T(8,128)(2,1)}, u32[]{:S(2)}, u32[]{:S(2)}) async-start(bf16[8,256,1024]{2,0,1:T(8,128)(2,1)} %copy.83), calls=%async_computation.1 | async-start | bytes 8388608 | tf_op jit(solution)/shard_map/all_to_all | solution.py:54
  423.1 3.4 copy-start.2
  423.1 3.4 copy-start.4
  435.4 85.4 %copy-start.7 = (s32[8,2,2]{0,2,1:T(2,128)S(1)}, s32[8,2,2]{0,2,1:T(2,128)}, u32[]{:S(2)}) copy-start(s32[8,2,2]{0,2,1:T(2,128)} %param.14) | copy-start | bytes 388
  513.5 98.0 %all-to-all-start.3 = ((bf16[8,256,1024]{2,0,1:T(8,128)(2,1)}), bf16[8,256,1024]{2,0,1:T(8,128)(2,1)}, u32[]{:S(2)}, u32[]{:S(2)}) async-start(bf16[8,256,1024]{2,0,1:T(8,128)(2,1)} %copy.91), calls=%async_computation.3 | async-start | bytes 8388608 | tf_op jit(solution)/shard_map/all_to_all | solution.py:38
  524.2 8.5 copy-start.1
  530.8 1.9 copy-start
  611.5 107.0 %all-to-all-start.2 = ((bf16[256,8,1024]{2,1,0:T(8,128)(2,1)}), bf16[256,8,1024]{2,1,0:T(8,128)(2,1)}, u32[]{:S(2)}, u32[]{:S(2)}) async-start(bf16[256,8,1024]{2,1,0:T(8,128)(2,1)} %copy.88), calls=%async_computation.2 | async-start | bytes 8388608 | tf_op jit(solution)/shard_map/all_to_all | solution.py:62
  718.5 98.0 %all-to-all-start.4 = ((bf16[256,8,1024]{2,1,0:T(8,128)(2,1)}), bf16[256,8,1024]{2,1,0:T(8,128)(2,1)}, u32[]{:S(2)}, u32[]{:S(2)}) async-start(bf16[256,8,1024]{2,1,0:T(8,128)(2,1)} %copy.96), calls=%async_computation.4 | async-start | bytes 8388608 | tf_op jit(solution)/shard_map/all_to_all | solution.py:45
  725.9 7.4 copy-start.3
where the time goes:
time: 894 us; the launch traced here: 885 us
  waiting for transfers between devices  368 us (41%)
  local copies, waits for them, and re-layouts  319 us (36%)
  blocking collectives  76.2 us (9%)
  starting transfers between devices  52.8 us (6%)
  matrix products  38 us (4%)
  other arithmetic  29.4 us (3%)
    gather x2, local copies, waits for them, and re-layouts, local(): looked_up = jnp.take(embed_table, every_id, axis=1)  239 us
    all_to_all x1, waiting for transfers between devices, local(): lax.all_to_all(grad_mixed_rows, 'seq', split_axis=1, concat_axis=0, tiled...  78 us
    all_to_all x1, waiting for transfers between devices, local(): lax.all_to_all(grad_row_cols, 'seq', split_axis=0, concat_axis=1, tiled=T...  78 us
    all_to_all x1, waiting for transfers between devices, local(): lax.all_to_all(looked_up, 'seq', split_axis=1, concat_axis=0, tiled=True)  77.2 us
    all_to_all x1, waiting for transfers between devices, local(): lax.all_to_all(mixed, 'seq', split_axis=0, concat_axis=1, tiled=True)  70.1 us
    all_to_all x1, waiting for transfers between devices, local(): lax.all_to_all(row_mixed, 'seq', split_axis=1, concat_axis=0, tiled=True)  64.7 us
    psum x1, blocking collectives, local(): grad_value_gain, grad_gate_gain = lax.psum((value_term, gate_term), 'seq')  43.5 us
    all_gather x1, blocking collectives, local(): every_id = lax.all_gather(token_ids, 'seq', axis=0, tiled=True)  32.7 us
  transfers between devices with their start and end apart: 5, of which 5 were waited for; matrix products, arithmetic and copies ran while one was open for 9% of the time, Pallas kernels for 0%

commit v1 on v0

v1 whole, which is shorter than its diff:
```python
import jax
import jax.numpy as jnp
from jax import lax
from jax.sharding import PartitionSpec as P


def expand_pattern(pattern, tile_size):
    return jnp.repeat(jnp.repeat(pattern, tile_size, axis=1), tile_size, axis=2).astype(
        jnp.bfloat16
    )


def make_local(devices):
    splits = 4 if devices % 4 == 0 else 1
    plane = devices // splits
    plane_groups = [[s * plane + p for p in range(plane)] for s in range(splits)]
    split_groups = [[s * plane + p for s in range(splits)] for p in range(plane)]

    def local(
        token_ids,
        embed_table,
        right_blocks,
        right_pattern,
        left_blocks,
        left_pattern,
        value_gain,
        gate_gain,
        cotangent,
    ):
        rows = right_blocks.shape[0]
        side = right_blocks.shape[1]
        channels = value_gain.shape[0]
        part = channels // splits
        held = splits * rows
        tile_size = side // right_pattern.shape[1]
        me = lax.axis_index("seq")
        my_split, my_place = me // plane, me % plane

        every_id = lax.all_gather(token_ids, "seq", axis=0, tiled=True)
        table = lax.all_gather(
            embed_table, "seq", axis=0, tiled=True, axis_index_groups=plane_groups
        )
        right_mask = expand_pattern(right_pattern, tile_size)
        left_mask = expand_pattern(left_pattern, tile_size)
        right_eff = lax.all_gather(
            right_blocks * right_mask, "seq", axis=0, tiled=True, axis_index_groups=split_groups
        )
        left_eff = lax.all_gather(
            left_blocks * left_mask, "seq", axis=0, tiled=True, axis_index_groups=split_groups
        )
        sent = cotangent.reshape(rows, splits, plane, rows, splits, part)
        sent = sent.transpose(4, 2, 1, 3, 0, 5).reshape(devices, held, rows, part)
        came = lax.all_to_all(sent, "seq", split_axis=0, concat_axis=0, tiled=True)
        grad_out = came.transpose(1, 0, 2, 3).reshape(held, side, part)

        row_ids = lax.dynamic_index_in_dim(
            every_id.reshape(splits, plane, rows, side), my_place, 1, keepdims=False
        ).reshape(-1)
        column_ids = (
            lax.dynamic_index_in_dim(
                every_id.reshape(side, splits, plane, rows), my_place, 2, keepdims=False
            )
            .reshape(side, held)
            .T.reshape(-1)
        )
        looked_up = jnp.take(table.T, jnp.concatenate([row_ids, column_ids]), axis=0, mode="clip")
        looked_up = looked_up.reshape(2, held, side, part)
        x_rows, x_columns = looked_up[0], looked_up[1]
        my_value_gain = lax.dynamic_slice_in_dim(value_gain, my_split * part, part)
        my_gate_gain = lax.dynamic_slice_in_dim(gate_gain, my_split * part, part)

        values = (x_rows.astype(jnp.float32) * my_value_gain).astype(jnp.bfloat16)
        row_mixed = jnp.einsum(
            "ikj,ijc->ikc", right_eff, values, preferred_element_type=jnp.float32
        ).astype(jnp.bfloat16)
        sent = row_mixed.reshape(splits, rows, splits, plane, rows, part)
        sent = sent.transpose(3, 2, 4, 0, 1, 5).reshape(plane, held, splits, rows, part)
        came = lax.all_to_all(
            sent, "seq", split_axis=0, concat_axis=0, tiled=True, axis_index_groups=plane_groups
        )
        column_view = came.transpose(1, 2, 0, 3, 4).reshape(held, side, part)

        mixed = jnp.einsum(
            "kai,kic->kac", left_eff, column_view, preferred_element_type=jnp.float32
        )
        inputs_f32 = x_columns.astype(jnp.float32)
        gate_value = jax.nn.sigmoid(inputs_f32 * my_gate_gain)
        gated = grad_out.astype(jnp.float32) * gate_value
        grad_mixed = gated.astype(jnp.bfloat16)
        product = gated * mixed
        value_term = jnp.sum(product, axis=(0, 1)) / my_value_gain
        gate_term = jnp.sum(product * (1.0 - gate_value) * inputs_f32, axis=(0, 1))

        grad_rows = jnp.einsum(
            "kai,kac->kic", left_eff, grad_mixed, preferred_element_type=jnp.float32
        ).astype(jnp.bfloat16)
        sent = grad_rows.reshape(held, splits, plane, rows, part).transpose(2, 0, 1, 3, 4)
        came = lax.all_to_all(
            sent, "seq", split_axis=0, concat_axis=0, tiled=True, axis_index_groups=plane_groups
        )
        grad_row_mixed = (
            came.reshape(plane, splits, rows, held, part)
            .transpose(3, 1, 0, 2, 4)
            .reshape(held, side, part)
        )
        left_part = jnp.einsum(
            "kac,kic->kai", grad_mixed, column_view, preferred_element_type=jnp.float32
        ).astype(jnp.bfloat16)

        def gathered_sum(terms, mask):
            came = lax.all_to_all(
                terms.reshape(splits, rows, side, side),
                "seq",
                split_axis=0,
                concat_axis=0,
                tiled=True,
                axis_index_groups=split_groups,
            )
            total = jnp.sum(came.astype(jnp.float32), axis=0)
            return (total * mask.astype(jnp.float32)).astype(jnp.bfloat16)

        grad_left = gathered_sum(left_part, left_mask)
        right_part = jnp.einsum(
            "ikc,ijc->ikj", grad_row_mixed, values, preferred_element_type=jnp.float32
        ).astype(jnp.bfloat16)
        grad_right = gathered_sum(right_part, right_mask)

        blank = jnp.zeros((2, channels), jnp.float32)
        terms = lax.dynamic_update_slice(
            blank, jnp.stack([value_term, gate_term]), (0, my_split * part)
        )
        totals = lax.psum(terms, "seq")
        return grad_right, grad_left, totals[0], totals[1]

    return local


def solution(mesh):
    return jax.shard_map(
        make_local(mesh.shape["seq"]),
        mesh=mesh,
        in_specs=(
            P(("groups", "seq")),
            P("seq", None),
            P("seq", None, None),
            P("seq", None, None),
            P("seq", None, None),
            P("seq", None, None),
            P(),
            P(),
            P(("groups", "seq"), None),
        ),
        out_specs=(
            P(("groups", "seq"), None, None),
            P(("groups", "seq"), None, None),
            P("groups"),
            P("groups"),
        ),
        check_vma=False,
    )
```

time: 894 us -> 605 us (0.68)
  waiting for transfers between devices: 368 us -> 155 us
  local copies, waits for them, and re-layouts: 319 us -> 136 us
  blocking collectives: 76.2 us -> 216 us
  starting transfers between devices: 52.8 us -> 32.9 us
  other arithmetic: 29.4 us -> 13.3 us
  between operations: 1.05 us -> 14 us
    all_to_all x5, waiting for transfers between devices: 368 us -> 115 us  [the longest x2 80.1 us: gathered_sum(): lax.all_to_all(terms.reshape(splits, rows, side, side), 'seq', split_axis...]
    gather x2 -> x1, local copies, waits for them, and re-layouts: 239 us -> 68.3 us  [local(): jnp.take(table.T, jnp.concatenate([row_ids, column_ids]), axis=0, mode='c...]
    all_gather x1, blocking collectives: 32.7 us -> 112 us  [local(): every_id = lax.all_gather(token_ids, 'seq', axis=0, tiled=True)]
    psum x1, blocking collectives: 43.5 us -> 104 us  [local(): totals = lax.psum(terms, 'seq')]
    convert_element_type x8 -> x0, local copies, waits for them, and re-layouts: 51.7 us -> none  [the longest x2 13.3 us: local(): mixed_rows.astype(jnp.float32)]
    all_gather x0 -> x3, waiting for transfers between devices: none -> 39.5 us  [the longest x1 39.5 us: local(): lax.all_gather(left_blocks * left_mask, 'seq', axis=0, tiled=True, axis_i...]
    all_gather x0 -> x1, local copies, waits for them, and re-layouts: none -> 20.6 us  [local(): lax.all_gather(embed_table, 'seq', axis=0, tiled=True, axis_index_groups=...]
    reshape x0 -> x5, local copies, waits for them, and re-layouts: none -> 20.4 us  [the longest x1 8.71 us: local(): sent = cotangent.reshape(rows, splits, plane, rows, splits, part)]
  transfers between devices with their start and end apart: 5 -> 8, of which waited for: 5 -> 3; matrix products, arithmetic and copies ran while one was open for 9% -> 29% of each run, Pallas kernels for 0% -> 0%
where the time goes in v1:
time: 605 us; the launch traced here: 601 us
  blocking collectives  216 us (36%)
  waiting for transfers between devices  155 us (26%)
  local copies, waits for them, and re-layouts  136 us (22%)
  matrix products  33.2 us (5%)
  starting transfers between devices  32.9 us (5%)
  between operations  14 us (2%)
  other arithmetic  13.3 us (2%)
    all_gather x1, blocking collectives, local(): every_id = lax.all_gather(token_ids, 'seq', axis=0, tiled=True)  112 us
    psum x1, blocking collectives, local(): totals = lax.psum(terms, 'seq')  104 us
    all_to_all x2, waiting for transfers between devices, gathered_sum(): lax.all_to_all(terms.reshape(splits, rows, side, side), 'seq', split_axis...  80.1 us
    gather x1, local copies, waits for them, and re-layouts, local(): jnp.take(table.T, jnp.concatenate([row_ids, column_ids]), axis=0, mode='c...  68.3 us
    all_gather x1, waiting for transfers between devices, local(): lax.all_gather(left_blocks * left_mask, 'seq', axis=0, tiled=True, axis_i...  39.5 us
    all_to_all x2, waiting for transfers between devices, local(): lax.all_to_all(sent, 'seq', split_axis=0, concat_axis=0, tiled=True, axis...  34.9 us
    all_gather x1, local copies, waits for them, and re-layouts, local(): lax.all_gather(embed_table, 'seq', axis=0, tiled=True, axis_index_groups=...  20.6 us
    all_to_all x2, starting transfers between devices, gathered_sum(): lax.all_to_all(terms.reshape(splits, rows, side, side), 'seq', split_axis...  16.2 us
  transfers between devices with their start and end apart: 8, of which 3 were waited for; matrix products, arithmetic and copies ran while one was open for 29% of the time, Pallas kernels for 0%

profile of v1, /device:TPU:12, one launch (start us, length us, event | category | flops | bytes accessed | tf_op | source)
XLA Modules:
  0.0 600.8 jit_solution(12276599546397243837)
XLA Ops:
  7.2 0.7 all-gather.6.cloned.1.call-update
  8.0 0.7 convert_element_type.94
  8.6 0.1 copy.40
  8.7 0.1 broadcast_in_dim.24
  8.8 2.5 broadcast_in_dim.25
  11.3 0.7 convert_element_type.96
  12.0 1.2 mul.53
  13.3 8.7 %copy.33 = bf16[8,4,8,8,4,256]{5,0,3,1,2,4:T(8,128)(2,1)} copy(bf16[8,4,8,8,4,256]{5,3,4,2,1,0:T(8,128)(2,1)} %bitcast.76) | data formatting | bytes 8388608 | tf_op jit(solution)/shard_map/reshape | solution.py:51
  22.0 6.1 %all-to-all-start = ((bf16[32,32,8,256]{3,2,1,0:T(8,128)(2,1)}), bf16[32,32,8,256]{3,2,1,0:T(8,128)(2,1)}, u32[]{:S(2)}, u32[]{:S(2)}) async-start(bf16[32,32,8,256]{3,2,1,0:T(8,128)(2,1)} %bitcast.73), calls=%async_computation | async-start | bytes 8388608 | tf_op jit(solution)/shard_map/all_to_all | solution.py:53
  28.1 0.1 copy.32
  28.2 0.1 broadcast_in_dim.21
  28.3 2.5 broadcast_in_dim.22
  30.8 0.7 convert_element_type.81
  31.5 2.4 mul.45
  34.0 112.1 %all_gather.14 = s32[65536]{0:T(1024)S(1)} all-gather(s32[2048]{0:T(1024)S(1)} %copy-done.3), channel_id=1, replica_groups=mesh['groups'=1,'seq'=32] {'seq'}, dimensions={0}, use_global_device_ids=true | all-gather | bytes 270336 | tf_op jit(solution)/shard_map/all_gather | solution.py:39
  146.1 3.6 reshape.81
  149.7 0.1 reshape.79
  149.8 2.9 constant_dynamic-slice_fusion
  152.8 0.4 copy.36
  153.3 0.1 dynamic_slice.17
  153.4 20.6 %copy.35 = bf16[256,30522]{0,1:T(8,128)(2,1)} copy(bf16[256,30522]{1,0:T(8,128)(2,1)} %all-gather.6.cloned.1.call-done) | data formatting | bytes 31254528 | tf_op jit(solution)/shard_map/all_gather | solution.py:40
  174.0 68.3 %gather_fusion = bf16[16384,256]{1,0:T(8,128)(2,1)} fusion(bf16[30522,256]{1,0:T(8,128)(2,1)} %bitcast.67, s32[16384]{0:T(1024)S(1)} %add_clamp_fusion), kind=kCustom, calls=%fused_computation | custom fusion | bytes 16842752 | tf_op jit(solution)/shard_map/jit(_take)/gather | solution.py:66
  242.4 5.8 fusion.18
  248.2 4.8 fusion.13
  253.0 5.4 copy.41
  258.4 5.8 all-to-all-start.3
  264.2 0.8 dynamic_slice.16
  264.9 39.5 %all-gather.4.cloned.1.call-done = bf16[32,256,256]{2,1,0:T(8,128)(2,1)} async-done(((bf16[8,256,256]{2,1,0:T(8,128)(2,1)}), bf16[32,256,256]{2,1,0:T(8,128)(2,1)}) %all-gather.4.cloned.1.call-update) | async-done | bytes 4194320 | tf_op jit(solution)/shard_map/all_gather | solution.py:48
  304.4 8.2 %convolution_convert_fusion.1 = bf16[32,256,256]{2,1,0:T(8,128)(2,1)S(1)} fusion(bf16[32,256,256]{2,1,0:T(8,128)(2,1)} %all-gather.4.cloned.1.call-done, f32[256]{0:T(256)S(1)} %dynamic_slice.16, bf16[32,256,256]{2,1,0:T(8,128)(2,1)} %bitcast.81, bf16[32,32,8,256]{3,2,1,0:T(8,128)(2,1)} %all-to-all-done), kind=kOutput, calls=%fused_computation.21 | convolution fusion | flops 1092616192 | bytes 16778240 | tf_op jit(solution)/shard_map/kai,kac->kic/dot_general | solution.py:94
  312.6 2.6 copy.58
  315.2 4.8 all-to-all-start.1
  320.0 2.8 copy.42
  322.8 1.9 copy-done.1
  324.7 8.1 %convolution_convert_fusion = bf16[32,256,256]{2,1,0:T(8,128)(2,1)} fusion(bf16[32,256,256]{2,1,0:T(8,128)(2,1)S(1)} %bitcast.77, f32[256]{0:T(256)S(1)} %dynamic_slice.16, bf16[32,256,256]{2,1,0:T(8,128)(2,1)} %bitcast.82, bf16[32,32,8,256]{3,2,1,0:T(8,128)(2,1)} %all-to-all-done), kind=kOutput, calls=%fused_computation.20 | convolution fusion | flops 1092616192 | bytes 16778240 | tf_op jit(solution)/shard_map/kac,kic->kai/dot_general | solution.py:106
  332.8 34.9 %all-to-all-done.1 = bf16[8,32,4,8,256]{4,3,2,1,0:T(8,128)(2,1)} async-done(((bf16[8,32,4,8,256]{4,3,2,1,0:T(8,128)(2,1)}), bf16[8,32,4,8,256]{4,3,2,1,0:T(8,128)(2,1)}, u32[]{:S(2)}, u32[]{:S(2)}) %all-to-all-start.1) | async-done | bytes 4194336 | tf_op jit(solution)/shard_map/all_to_all | solution.py:98
  367.7 8.0 %all-to-all-start.4 = ((bf16[4,8,256,256]{3,2,1,0:T(8,128)(2,1)}), bf16[4,8,256,256]{3,2,1,0:T(8,128)(2,1)}, u32[]{:S(2)}, u32[]{:S(2)}) async-start(bf16[4,8,256,256]{3,2,1,0:T(8,128)(2,1)} %bitcast.79), calls=%async_computation.4 | async-start | bytes 8388608 | tf_op jit(solution)/shard_map/all_to_all | solution.py:111
  375.7 4.7 copy.39
  380.5 3.3 fusion.10
  383.7 80.1 %all-to-all-done.4 = bf16[4,8,256,256]{3,2,1,0:T(8,128)(2,1)} async-done(((bf16[4,8,256,256]{3,2,1,0:T(8,128)(2,1)}), bf16[4,8,256,256]{3,2,1,0:T(8,128)(2,1)}, u32[]{:S(2)}, u32[]{:S(2)}) %all-to-all-start.4) | async-done | bytes 4194336 | tf_op jit(solution)/shard_map/all_to_all | solution.py:111
  463.8 8.2 %all-to-all-start.2 = ((bf16[4,8,256,256]{3,2,1,0:T(8,128)(2,1)}), bf16[4,8,256,256]{3,2,1,0:T(8,128)(2,1)}, u32[]{:S(2)}, u32[]{:S(2)}) async-start(bf16[4,8,256,256]{3,2,1,0:T(8,128)(2,1)} %bitcast.70), calls=%async_computation.2 | async-start | bytes 8388608 | tf_op jit(solution)/shard_map/all_to_all | solution.py:111
  472.0 8.8 %multiply_reduce_fusion = (f32[256]{0:T(256)S(1)}, f32[256]{0:T(256)S(1)}) fusion(f32[256]{0:T(256)S(1)} %dynamic_slice.16, bf16[16384,256]{1,0:T(8,128)(2,1)} %gather_fusion, bf16[32,256,256]{2,1,0:T(8,128)(2,1)} %all-gather.4.cloned.1.call-done, bf16[32,256,256]{2,1,0:T(8,128)(2,1)} %bitcast.78, bf16[32,32,8,256]{3,2,1,0:T(8,128)(2,1)} %all-to-all-done), kind=kOutput, calls=%fused_computation.15 | convolution fusion | flops 1101004288 | bytes 16780288 | tf_op jit(solution)/shard_map/kai,kic->kac/dot_general | solution.py:83
  480.7 0.1 dynamic-slice_divide_fusion
  480.8 104.0 %psum.7 = f32[2,1024]{1,0:T(2,128)S(1)} all-reduce(f32[2,1024]{1,0:T(2,128)S(1)} %maximum_dynamic-update-slice_fusion), channel_id=1, replica_groups=mesh['groups'=1,'seq'=32] {'seq'}, use_global_device_ids=true, to_apply=%region_4.5 | all-reduce | flops 2048 | bytes 16384 | tf_op jit(solution)/shard_map/psum | solution.py:132
  584.8 0.6 fusion.19
  585.4 3.1 convert_reduce_fusion
  588.6 1.3 multiply_convert_fusion
  589.9 3.1 convert_reduce_fusion.1
  593.0 1.3 multiply_convert_fusion.1
  (28 shorter events, 0.3 us)
Async XLA Ops:
  7.2 4.8 copy-start.2
  7.2 146.2 %all-gather.6.cloned.1.call-start = ((), (), s32[]{:S(2)}) async-start(), calls=%async_computation.6 | async-start | bytes 17620992 | tf_op jit(solution)/shard_map/all_gather | solution.py:40
  7.9 240.3 %all-gather.8.cloned.1.call-start = ((), (), s32[]{:S(2)}) async-start(), calls=%async_computation.7 | async-start | bytes 5242880 | tf_op jit(solution)/shard_map/all_gather | solution.py:45
  22.0 6.1 %copy-start.4 = (s32[8,2,2]{0,2,1:T(2,128)S(1)}, s32[8,2,2]{0,2,1:T(2,128)}, u32[]{:S(2)}) copy-start(s32[8,2,2]{0,2,1:T(2,128)} %param.14) | copy-start | bytes 388
  22.0 236.4 %all-to-all-start = ((bf16[32,32,8,256]{3,2,1,0:T(8,128)(2,1)}), bf16[32,32,8,256]{3,2,1,0:T(8,128)(2,1)}, u32[]{:S(2)}, u32[]{:S(2)}) async-start(bf16[32,32,8,256]{3,2,1,0:T(8,128)(2,1)} %bitcast.73), calls=%async_computation | async-start | bytes 8388608 | tf_op jit(solution)/shard_map/all_to_all | solution.py:53
  28.1 276.4 %all-gather.4.cloned.1.call-start = ((), (), s32[]{:S(2)}) async-start(), calls=%async_computation.5 | async-start | bytes 5242880 | tf_op jit(solution)/shard_map/all_gather | solution.py:48
  28.2 5.8 copy-start.3
  34.0 119.3 %copy-start.5 = (f32[1024]{0:T(1024)S(1)}, f32[1024]{0:T(1024)}, u32[]{:S(2)}) copy-start(f32[1024]{0:T(1024)} %param.15) | copy-start | bytes 12292
  258.4 56.8 %all-to-all-start.3 = ((bf16[8,32,4,8,256]{4,3,2,1,0:T(8,128)(2,1)}), bf16[8,32,4,8,256]{4,3,2,1,0:T(8,128)(2,1)}, u32[]{:S(2)}, u32[]{:S(2)}) async-start(bf16[8,32,4,8,256]{4,3,2,1,0:T(8,128)(2,1)} %bitcast.74), calls=%async_computation.3 | async-start | bytes 8388608 | tf_op jit(solution)/shard_map/all_to_all | solution.py:78
  315.2 52.5 %all-to-all-start.1 = ((bf16[8,32,4,8,256]{4,3,2,1,0:T(8,128)(2,1)}), bf16[8,32,4,8,256]{4,3,2,1,0:T(8,128)(2,1)}, u32[]{:S(2)}, u32[]{:S(2)}) async-start(bf16[8,32,4,8,256]{4,3,2,1,0:T(8,128)(2,1)} %bitcast.75), calls=%async_computation.1 | async-start | bytes 8388608 | tf_op jit(solution)/shard_map/all_to_all | solution.py:98
  322.8 1.9 copy-start.1
  367.7 96.1 %all-to-all-start.4 = ((bf16[4,8,256,256]{3,2,1,0:T(8,128)(2,1)}), bf16[4,8,256,256]{3,2,1,0:T(8,128)(2,1)}, u32[]{:S(2)}, u32[]{:S(2)}) async-start(bf16[4,8,256,256]{3,2,1,0:T(8,128)(2,1)} %bitcast.79), calls=%async_computation.4 | async-start | bytes 8388608 | tf_op jit(solution)/shard_map/all_to_all | solution.py:111
  375.7 4.7 copy-start
  463.8 126.1 %all-to-all-start.2 = ((bf16[4,8,256,256]{3,2,1,0:T(8,128)(2,1)}), bf16[4,8,256,256]{3,2,1,0:T(8,128)(2,1)}, u32[]{:S(2)}, u32[]{:S(2)}) async-start(bf16[4,8,256,256]{3,2,1,0:T(8,128)(2,1)} %bitcast.70), calls=%async_computation.2 | async-start | bytes 8388608 | tf_op jit(solution)/shard_map/all_to_all | solution.py:111
Sparse Core Ops, SparseCore 0:
  9.9 131.4 all-gather.5
  143.6 79.3 all-gather.7
  225.1 79.2 all-gather.3
